TPU v7x, 256 devices: a whole 4x4x8 slice. The times are simulated.
256 devices in a mesh: view: 64 (over x, z, core), pix: 4 (over y).
Axes of the slice: x: 4, y: 4, z: 8, core: 2. Of those that a mesh axis runs over, the one named last changes fastest.
Arguments:
- target_tokens: bfloat16 [32768, 1024], P(('view', 'pix')), may hold values from -6 to 6
- input_tokens: bfloat16 [32768, 1024], P(('view', 'pix')), may hold values from -6 to 6
- w_query: bfloat16 [1024, 1024], P(None, 'pix')
- w_key: bfloat16 [1024, 1024], P(None, 'pix'), may hold values from -0.1875 to 0.1875
- w_value: bfloat16 [1024, 1024], P(None, 'pix'), may hold values from -0.1875 to 0.1875
- w_out: bfloat16 [1024, 1024], P('pix'), may hold values from -0.75 to 0.75
- table: int32 [256, 8], replicated, may hold values from 0 to 63, all different within a row; in each aligned block of 4 rows (0 to 3, 4 to 7, ...) at most 2 rows name the same one
- table_block: int32 [256, 8], replicated, may hold values from 0 to 3
- counts: int32 [256], P('view'), may hold values from 1 to 8
Outputs:
- output: bfloat16 [32768, 1024], P(('view', 'pix'))
Inputs may be any that keep to these rules, and one draw needn't show every extreme that they name: `table`: the entries of one row name different input views; within the rows of one target view (aligned blocks of 4 rows) no input view is named by more than 2 entries, counting all 8 columns.
All inputs are finite; a program needn't handle non-finite values.
Results may differ from a plain program's by a relative error of at most 0.0095.
The roundings to bfloat16 on the way count: a program that leaves them out, or rounds other values in their place, can miss the bound.
Values may be sent and summed in bfloat16 or wider, within the bound.
A program may use at most 128 MiB of HBM per device.

v0:
```python
import jax
import jax.numpy as jnp
from jax import lax
from jax.sharding import PartitionSpec as P

HEAD_DIM = 64
VIEW_TOK = 512
BLOCK = 128


def normalize(tokens):
    source = tokens.astype(jnp.float32)
    center = source - jnp.mean(source, axis=1, keepdims=True)
    spread = jnp.mean(center * center, axis=1, keepdims=True)
    return (center * lax.rsqrt(spread + 1e-05)).astype(jnp.bfloat16)


def body(target_tokens, input_tokens, w_query, w_key, w_value, w_out, table, table_block, counts):
    view_count = lax.axis_size("view")
    head_cols = w_query.shape[1]
    local_heads = head_cols // HEAD_DIM
    view_blocks = VIEW_TOK // BLOCK
    list_length = table.shape[1]
    capacity = max(2, (view_blocks * list_length + view_count - 1) // view_count)
    normed = jnp.stack([normalize(target_tokens), normalize(input_tokens)])
    piece = lax.all_gather(normed, "pix", axis=1, tiled=True)
    queries = jnp.dot(piece[0], w_query, preferred_element_type=jnp.float32)
    keys_new = jnp.dot(piece[1], w_key, preferred_element_type=jnp.float32)
    values_new = jnp.dot(piece[1], w_value, preferred_element_type=jnp.float32)
    qkv_rows = jnp.concatenate([queries, keys_new, values_new], axis=1).astype(jnp.bfloat16)
    query_rows = qkv_rows[:, :head_cols]
    kv_rows = qkv_rows[:, head_cols:]
    block_width = BLOCK * 2 * head_cols
    kv_blocks = kv_rows.reshape(view_blocks, block_width)
    own_view = lax.axis_index("view")
    entry_count = view_blocks * list_length
    entries = table.reshape(view_count, entry_count)
    entry_blocks = table_block.reshape(view_count, entry_count)
    matched = (entries == own_view).astype(jnp.int32)
    ranks = jnp.cumsum(matched, axis=1) - matched
    slot_ids = jnp.arange(capacity, dtype=jnp.int32)
    picked = matched[:, None, :] * (ranks[:, None, :] == slot_ids[None, :, None]).astype(jnp.int32)
    chosen = jnp.sum(picked * entry_blocks[:, None, :], axis=2)
    outgoing = jnp.take(kv_blocks, chosen.reshape(-1), axis=0).reshape(
        view_count, capacity, block_width
    )
    received = lax.all_to_all(outgoing, "view", split_axis=0, concat_axis=0, tiled=True)
    own_sources = lax.dynamic_slice_in_dim(entries, own_view, 1, 0)[0]
    positions = jnp.arange(entry_count, dtype=jnp.int32)
    earlier = (own_sources[:, None] == own_sources[None, :]) & (
        positions[None, :] < positions[:, None]
    )
    own_ranks = jnp.sum(earlier.astype(jnp.int32), axis=1)
    slot_index = own_sources * capacity + own_ranks
    listed = jnp.take(received.reshape(view_count * capacity, block_width), slot_index, axis=0)
    listed = listed.reshape(view_blocks, list_length * BLOCK, 2, local_heads, HEAD_DIM)
    key_rows = listed[:, :, 0]
    value_rows = listed[:, :, 1]
    query_blocks = query_rows.reshape(view_blocks, BLOCK, local_heads, HEAD_DIM)
    scores = jnp.einsum(
        "bqhd,bkhd->bhqk", query_blocks, key_rows, preferred_element_type=jnp.float32
    )
    scores = scores * HEAD_DIM ** (-0.5)
    live = (jnp.arange(list_length * BLOCK, dtype=jnp.int32) // BLOCK)[None, :] < counts[:, None]
    scores = jnp.where(live[:, None, None, :], scores, -1e30)
    peak = jnp.max(scores, axis=3, keepdims=True)
    weights = jnp.exp(scores - peak)
    probs = (weights / jnp.sum(weights, axis=3, keepdims=True)).astype(jnp.bfloat16)
    attended = jnp.einsum("bhqk,bkhd->bqhd", probs, value_rows, preferred_element_type=jnp.float32)
    attended = attended.astype(jnp.bfloat16).reshape(view_blocks * BLOCK, head_cols)
    mixed = lax.psum_scatter(
        jnp.dot(attended, w_out, preferred_element_type=jnp.float32),
        "pix",
        scatter_dimension=0,
        tiled=True,
    )
    return (target_tokens.astype(jnp.float32) + mixed).astype(jnp.bfloat16)


def solution(mesh):
    placed = (
        P(("view", "pix"), None),
        P(("view", "pix"), None),
        P(None, "pix"),
        P(None, "pix"),
        P(None, "pix"),
        P("pix", None),
        P(),
        P(),
        P("view"),
    )
    return jax.shard_map(
        body, mesh=mesh, in_specs=placed, out_specs=P(("view", "pix"), None), check_vma=False
    )
```

profile of v0, /device:TPU:1, one launch (start us, length us, event | category | flops | bytes accessed | tf_op | source)
XLA Modules:
  0.0 604.1 jit_solution(6125706127332962466)
XLA Ops:
  6.5 0.0 copy-start
  6.5 0.0 copy-start.2
  6.5 0.0 copy-start.4
  6.5 0.0 copy-start.5
  6.5 0.0 all-gather.2.cloned.1.call-start
  6.6 1.2 convert_reduce_fusion.1
  7.8 1.2 fusion.17
  8.9 1.1 convert_reduce_fusion
  10.0 1.2 fusion.15
  11.2 1.3 fusion.24
  12.5 0.8 pad_maximum_fusion
  13.3 0.0 all-gather.2.cloned.1.call-update
  13.3 0.8 copy.19
  14.2 0.1 reshape.186
  14.3 0.1 copy.21
  14.4 0.2 reduce_window_sum.11
  14.6 0.1 copy.20
  14.6 0.0 copy-done.2
  14.6 0.1 copy.22
  14.8 0.1 mul.73
  14.9 0.1 copy.23
  15.0 0.1 copy.26
  15.1 0.1 copy.24
  15.2 0.1 reshape.188
  15.4 35.3 %all-gather.2.cloned.1.call-done = bf16[2,512,1024]{2,1,0:T(8,128)(2,1)} async-done(((bf16[2,128,1024]{2,1,0:T(8,128)(2,1)}), bf16[2,512,1024]{2,1,0:T(8,128)(2,1)}) %all-gather.2.cloned.1.call-update) | async-done | bytes 2097168 | tf_op jit(solution)/shard_map/all_gather | solution.py:26
  50.7 0.0 copy-done.4
  50.7 1.7 convolution_convert_fusion.1
  52.4 0.0 copy-done.5
  52.4 1.7 convolution_convert_fusion.2
  54.2 0.2 copy.25
  54.4 0.4 reshape.187
  54.8 17.5 %gather_fusion = bf16[128,65536]{1,0:T(8,128)(2,1)} fusion(bf16[4,65536]{1,0:T(4,128)(2,1)S(1)} %reshape.187, s32[1024]{0:T(1024)S(1)} %pad_clamp_fusion.1), kind=kCustom, calls=%fused_computation | custom fusion | bytes 33554944 | tf_op jit(solution)/shard_map/jit(_take)/gather | solution.py:44
  72.3 19.9 %gather.13 = bf16[64,2,65536]{2,1,0:T(2,128)(2,1)} reshape(bf16[128,65536]{1,0:T(8,128)(2,1)} %gather_fusion) | data formatting | bytes 33554432 | tf_op jit(solution)/shard_map/jit(_take)/gather | solution.py:44
  92.2 19.3 %broadcast_select_fusion = bf16[64,2,65536]{2,1,0:T(2,128)(2,1)} fusion(bf16[64,2,65536]{2,1,0:T(2,128)(2,1)} %gather.13, pred[64,2]{1,0:T(8,128)(4,1)S(1)} %copy.24), kind=kLoop, calls=%fused_computation.3 | loop fusion | flops 8388608 | bytes 33554560 | tf_op jit(solution)/shard_map/jit(_take)/select_n | solution.py:44
  111.5 0.0 copy-start.3
  111.5 0.0 copy-start.6
  111.5 11.0 %all-to-all-start = ((bf16[64,2,65536]{2,1,0:T(2,128)(2,1)}), bf16[64,2,65536]{2,1,0:T(2,128)(2,1)}, u32[]{:S(2)}, u32[]{:S(2)}) async-start(bf16[64,2,65536]{2,1,0:T(2,128)(2,1)} %broadcast_select_fusion), calls=%async_computation | async-start | bytes 33554432 | tf_op jit(solution)/shard_map/all_to_all | solution.py:47
  122.5 0.0 reduce-scatter.2.cloned.1.call-start
  122.6 0.2 convert_reduce_fusion.2
  122.8 0.1 reduce_sum.68
  122.8 0.1 mul.70
  122.9 0.1 broadcast_bitcast_fusion
  123.1 0.0 copy-done.3
  123.1 0.1 broadcast_compare_fusion
  123.2 0.0 copy-done.6
  123.2 1.7 convolution_convert_fusion
  124.8 0.2 reshape.208
  125.1 363.0 %all-to-all-done = bf16[64,2,65536]{2,1,0:T(2,128)(2,1)} async-done(((bf16[64,2,65536]{2,1,0:T(2,128)(2,1)}), bf16[64,2,65536]{2,1,0:T(2,128)(2,1)}, u32[]{:S(2)}, u32[]{:S(2)}) %all-to-all-start) | async-done | bytes 16777248 | tf_op jit(solution)/shard_map/all_to_all | solution.py:47
  488.0 19.8 %reshape.189 = bf16[128,65536]{1,0:T(8,128)(2,1)} reshape(bf16[64,2,65536]{2,1,0:T(2,128)(2,1)} %all-to-all-done) | data formatting | bytes 33554432 | tf_op jit(solution)/shard_map/reshape | solution.py:55
  507.8 16.6 %gather_fusion.1 = bf16[32,65536]{1,0:T(8,128)(2,1)} fusion(bf16[128,65536]{1,0:T(8,128)(2,1)} %reshape.189, s32[1024]{0:T(1024)S(1)} %pad_clamp_fusion), kind=kCustom, calls=%fused_computation.1 | custom fusion | bytes 8388736 | tf_op jit(solution)/shard_map/jit(_take)/gather | solution.py:55
  524.5 10.4 %gather.15 = bf16[4,1024,2,4,64]{4,3,2,1,0:T(4,128)(2,1)} reshape(bf16[32,65536]{1,0:T(8,128)(2,1)} %gather_fusion.1) | data formatting | bytes 8388608 | tf_op jit(solution)/shard_map/jit(_take)/gather | solution.py:55
  534.8 12.8 %copy.27 = bf16[4,1024,2,4,64]{1,4,3,0,2:T(8,128)(2,1)} copy(bf16[4,1024,2,4,64]{4,3,2,1,0:T(4,128)(2,1)} %gather.15) | data formatting | bytes 8388608 | tf_op jit(solution)/shard_map/jit(_take)/gather | solution.py:55
  547.6 4.5 broadcast_select_fusion.1
  552.1 7.6 %fusion.38 = (f32[4,4,128]{2,1,0:T(4,128)S(1)}, f32[4,4,128,1024]{3,2,1,0:T(8,128)}) fusion(pred[4,1024]{1,0:T(4,128)(4,1)S(1)} %broadcast_compare_fusion, bf16[4,1024,2,4,64]{1,4,3,0,2:T(8,128)(2,1)} %broadcast_select_fusion.1, bf16[4,128,4,64]{3,2,1,0:T(4,128)(2,1)S(1)} %reshape.208), kind=kOutput, calls=%fused_computation.83 | convolution fusion | flops 276825088 | bytes 10760192 | tf_op jit(solution)/shard_map/sub | solution.py:67
  559.7 5.7 fusion.10
  565.4 0.0 copy-start.1
  565.4 0.2 copy.30
  565.6 0.0 copy-done
  565.6 1.8 fusion.26
  567.4 0.0 reduce-scatter.2.cloned.1.call-update
  567.5 28.0 %reduce-scatter.2.cloned.1.call-done = f32[128,1024]{1,0:T(8,128)} async-done(((f32[512,1024]{1,0:T(8,128)}), f32[128,1024]{1,0:T(8,128)}) %reduce-scatter.2.cloned.1.call-update) | async-done | bytes 524304 | tf_op jit(solution)/shard_map/reduce_scatter | solution.py:71
  595.4 0.0 copy-done.1
  595.4 1.8 fusion.19
  (17 shorter events, 0.2 us)
Async XLA Ops:
  6.5 559.1 %copy-start = (bf16[256,1024]{1,0:T(8,128)(2,1)S(1)}, bf16[256,1024]{1,0:T(8,128)(2,1)}, u32[]{:S(2)}) copy-start(bf16[256,1024]{1,0:T(8,128)(2,1)} %param.14) | copy-start | bytes 1572868
  6.5 8.1 %copy-start.2 = (s32[256,8]{0,1:T(8,128)S(1)}, s32[256,8]{0,1:T(8,128)}, u32[]{:S(2)}) copy-start(s32[256,8]{0,1:T(8,128)} %param.16) | copy-start | bytes 24580
  6.5 44.2 %copy-start.4 = (bf16[1024,256]{1,0:T(8,128)(2,1)S(1)}, bf16[1024,256]{1,0:T(8,128)(2,1)}, u32[]{:S(2)}) copy-start(bf16[1024,256]{1,0:T(8,128)(2,1)} %param.13) | copy-start | bytes 1572868
  6.5 45.9 %copy-start.5 = (bf16[1024,256]{1,0:T(8,128)(2,1)S(1)}, bf16[1024,256]{1,0:T(8,128)(2,1)}, u32[]{:S(2)}) copy-start(bf16[1024,256]{1,0:T(8,128)(2,1)} %param.12) | copy-start | bytes 1572868
  6.5 44.2 %all-gather.2.cloned.1.call-start = ((), (), s32[]{:S(2)}) async-start(), calls=%async_computation.2 | async-start | bytes 2621440 | tf_op jit(solution)/shard_map/all_gather | solution.py:26
  111.5 11.6 %copy-start.3 = (s32[4]{0:T(128)S(1)}, s32[4]{0:T(128)}, u32[]{:S(2)}) copy-start(s32[4]{0:T(128)} %param.17) | copy-start | bytes 52
  111.5 11.7 %copy-start.6 = (bf16[1024,256]{1,0:T(8,128)(2,1)S(1)}, bf16[1024,256]{1,0:T(8,128)(2,1)}, u32[]{:S(2)}) copy-start(bf16[1024,256]{1,0:T(8,128)(2,1)} %param.11) | copy-start | bytes 1572868
  111.5 376.5 %all-to-all-start = ((bf16[64,2,65536]{2,1,0:T(2,128)(2,1)}), bf16[64,2,65536]{2,1,0:T(2,128)(2,1)}, u32[]{:S(2)}, u32[]{:S(2)}) async-start(bf16[64,2,65536]{2,1,0:T(2,128)(2,1)} %broadcast_select_fusion), calls=%async_computation | async-start | bytes 33554432 | tf_op jit(solution)/shard_map/all_to_all | solution.py:47
  122.5 472.9 %reduce-scatter.2.cloned.1.call-start = ((), (), s32[]{:S(2)}) async-start(), calls=%async_computation.3 | async-start | bytes 2621440 | tf_op jit(solution)/shard_map/reduce_scatter | solution.py:71
  565.4 30.0 %copy-start.1 = (bf16[128,1024]{1,0:T(8,128)(2,1)S(1)}, bf16[128,1024]{1,0:T(8,128)(2,1)}, u32[]{:S(2)}) copy-start(bf16[128,1024]{1,0:T(8,128)(2,1)} %param.9) | copy-start | bytes 786436
Sparse Core Ops, SparseCore 0:
  13.5 37.2 all-gather.1
  567.6 27.7 reduce-scatter.1
where the time goes:
time: 606 us; the launch traced here: 604 us
  waiting for transfers between devices  426 us (70%)
  local copies, waits for them, and re-layouts  99.9 us (16%)
  other arithmetic  33 us (5%)
  matrix products  20.1 us (3%)
  between operations  13.6 us (2%)
  starting transfers between devices  11.1 us (2%)
    all_to_all x1, waiting for transfers between devices, body(): lax.all_to_all(outgoing, 'view', split_axis=0, concat_axis=0, tiled=True)  363 us
    gather x3, local copies, waits for them, and re-layouts, body(): jnp.take(received.reshape(view_count * capacity, block_width), slot_index...  39.8 us
    gather x2, local copies, waits for them, and re-layouts, body(): jnp.take(kv_blocks, chosen.reshape(-1), axis=0)  37.4 us
    all_gather x1, waiting for transfers between devices, body(): piece = lax.all_gather(normed, 'pix', axis=1, tiled=True)  35.3 us
    reduce_scatter x1, waiting for transfers between devices, body(): lax.psum_scatter(jnp.dot(attended, w_out, preferred_element_type=jnp.floa...  28 us
    reshape x1, local copies, waits for them, and re-layouts, body(): received.reshape(view_count * capacity, block_width)  19.8 us
    select_n x2, other arithmetic, body(): jnp.take(kv_blocks, chosen.reshape(-1), axis=0)  19.3 us
  transfers between devices with their start and end apart: 3, of which 3 were waited for; matrix products, arithmetic and copies ran while one was open for 1% of the time, Pallas kernels for 0%

commit v1 on v0

v1 whole, which is shorter than its diff:
```python
import jax
import jax.numpy as jnp
from jax import lax
from jax.experimental import pallas as pl
from jax.experimental.pallas import tpu as pltpu
from jax.sharding import Mesh, PartitionSpec as P

D = 1024
HEAD_DIM = 64
BLOCK = 128
LIST_LEN = 8
PIX = 4
GROUP = ("x", "core", "pix")


def normalize(tokens):
    source = tokens.astype(jnp.float32)
    center = source - jnp.mean(source, axis=1, keepdims=True)
    spread = jnp.mean(center * center, axis=1, keepdims=True)
    return (center * lax.rsqrt(spread + 1e-05)).astype(jnp.bfloat16)


def attend_kernel(count_ref, target_ref, listed_ref, wq_ref, wk_ref, wv_ref, wo_ref, out_ref, normed, total):
    step = pl.program_id(0)

    @pl.when(step == 0)
    def _():
        normed[...] = normalize(target_ref[...])

    listed = listed_ref[...]
    query = jnp.dot(normed[...], wq_ref[0], preferred_element_type=jnp.float32).astype(jnp.bfloat16)
    key = jnp.dot(listed, wk_ref[0], preferred_element_type=jnp.float32).astype(jnp.bfloat16)
    value = jnp.dot(listed, wv_ref[0], preferred_element_type=jnp.float32).astype(jnp.bfloat16)
    columns = lax.broadcasted_iota(jnp.int32, (1, LIST_LEN * BLOCK), 1)
    live = columns < count_ref[0] * BLOCK
    heads = []
    for h in range(query.shape[1] // HEAD_DIM):
        part = slice(h * HEAD_DIM, (h + 1) * HEAD_DIM)
        scores = lax.dot_general(
            query[:, part], key[:, part], (((1,), (1,)), ((), ())), preferred_element_type=jnp.float32
        )
        scores = jnp.where(live, scores * HEAD_DIM ** (-0.5), -1e30)
        peak = jnp.max(scores, axis=1, keepdims=True)
        weights = jnp.exp(scores - peak)
        probs = (weights * (1.0 / jnp.sum(weights, axis=1, keepdims=True))).astype(jnp.bfloat16)
        heads.append(jnp.dot(probs, value[:, part], preferred_element_type=jnp.float32).astype(jnp.bfloat16))
    attended = jnp.concatenate(heads, axis=1)
    mixed = jnp.dot(attended, wo_ref[0], preferred_element_type=jnp.float32)

    @pl.when(step == 0)
    def _():
        total[...] = mixed

    @pl.when(step > 0)
    def _():
        total[...] += mixed

    @pl.when(step == pl.num_programs(0) - 1)
    def _():
        out_ref[...] = (target_ref[...].astype(jnp.float32) + total[...]).astype(jnp.bfloat16)


def attend(count, target, listed, wq, wk, wv, wo):
    cols = D // PIX
    whole = lambda shape: pl.BlockSpec(shape, lambda i: (0, 0))
    return pl.pallas_call(
        attend_kernel,
        grid=(PIX,),
        out_shape=jax.ShapeDtypeStruct((BLOCK, D), jnp.bfloat16),
        in_specs=[
            pl.BlockSpec(memory_space=pltpu.SMEM),
            whole((BLOCK, D)),
            whole((LIST_LEN * BLOCK, D)),
            pl.BlockSpec((1, D, cols), lambda i: (i, 0, 0)),
            pl.BlockSpec((1, D, cols), lambda i: (i, 0, 0)),
            pl.BlockSpec((1, D, cols), lambda i: (i, 0, 0)),
            pl.BlockSpec((1, cols, D), lambda i: (i, 0, 0)),
        ],
        out_specs=whole((BLOCK, D)),
        scratch_shapes=[pltpu.VMEM((BLOCK, D), jnp.bfloat16), pltpu.VMEM((BLOCK, D), jnp.float32)],
        compiler_params=pltpu.CompilerParams(vmem_limit_bytes=48 * 1024 * 1024),
        cost_estimate=pl.CostEstimate(flops=5_400_000_000, bytes_accessed=11 << 20, transcendentals=2 << 20),
    )(count, target, listed, wq, wk, wv, wo)


def body(target_tokens, input_tokens, w_query, w_key, w_value, w_out, table, table_block, counts):
    x, z, core, y = (lax.axis_index(name) for name in ("x", "z", "core", "pix"))
    nx, nz, nc = (lax.axis_size(name) for name in ("x", "z", "core"))
    members = nx * nc * PIX
    normed = normalize(input_tokens)
    pieces = normed.reshape(nx * nc, 16, PIX, D // PIX).transpose(0, 2, 1, 3).reshape(members, 16, D // PIX)
    spread = lax.all_to_all(pieces, GROUP, split_axis=0, concat_axis=0, tiled=True)
    held = lax.all_gather(spread, "z", axis=0, tiled=True)
    weights = [lax.all_gather(w, "pix", axis=0, tiled=False) for w in (w_query, w_key, w_value, w_out)]
    place = ((table // 2) % nz) * members + ((table // (2 * nz)) * nc + table % nc) * PIX + table_block
    place = place.reshape(nx, nz, nc * PIX, LIST_LEN)
    wanted = lax.dynamic_index_in_dim(place, z, 1, keepdims=False).reshape(-1)
    outgoing = jnp.take(held, wanted, axis=0).reshape(members, LIST_LEN, 16, D // PIX)
    arrived = lax.all_to_all(outgoing, GROUP, split_axis=0, concat_axis=0, tiled=True)
    listed = arrived.reshape(nx * nc, PIX, LIST_LEN, 16, D // PIX).transpose(2, 0, 3, 1, 4)
    listed = listed.reshape(LIST_LEN * BLOCK, D)
    count = lax.dynamic_slice_in_dim(counts, y, 1, 0)
    return attend(count, target_tokens, listed, *weights)


def solution(mesh):
    views = ("x", "z", "core")
    fine = Mesh(mesh.devices.reshape(4, 8, 2, 4), ("x", "z", "core", "pix"))
    placed = (
        P((*views, "pix"), None),
        P((*views, "pix"), None),
        P(None, "pix"),
        P(None, "pix"),
        P(None, "pix"),
        P("pix", None),
        P(),
        P(),
        P(views),
    )
    return jax.shard_map(
        body, mesh=fine, in_specs=placed, out_specs=P((*views, "pix"), None), check_vma=False
    )
```

time: 606 us -> 251 us (0.41)
  waiting for transfers between devices: 426 us -> 178 us
  local copies, waits for them, and re-layouts: 99.9 us -> 8.45 us
  other arithmetic: 33 us -> 5.05 us
  matrix products: 20.1 us -> 0 us
  Pallas kernels: 0 us -> 17.3 us
  blocking collectives: 0 us -> 17.3 us
    all_to_all x1, waiting for transfers between devices: 363 us -> 29.8 us  [body(): lax.all_to_all(outgoing, GROUP, split_axis=0, concat_axis=0, tiled=True)]
    all_gather x1 -> x5, waiting for transfers between devices: 35.3 us -> 146 us  [the longest x4 112 us: body(): lax.all_gather(w, 'pix', axis=0, tiled=False)]
    gather x5 -> x1, local copies, waits for them, and re-layouts: 77.1 us -> 2.34 us  [body(): jnp.take(held, wanted, axis=0).reshape(members, LIST_LEN, 16, D // PIX)]
    reduce_scatter x1 -> x0, waiting for transfers between devices: 28 us -> none  [body(): lax.psum_scatter(jnp.dot(attended, w_out, preferred_element_type=jnp.floa...]
    select_n x5 -> x2, other arithmetic: 23.9 us -> 1.6 us  [body(): jnp.take(held, wanted, axis=0).reshape(members, LIST_LEN, 16, D // PIX)]
    reshape x5 -> x4, local copies, waits for them, and re-layouts: 20.6 us -> 0.43 us  [the longest x1 0.18 us: body(): normed.reshape(nx * nc, 16, PIX, D // PIX).transpose(0, 2, 1, 3)]
    all_to_all x0 -> x1, blocking collectives: none -> 17.3 us  [body(): lax.all_to_all(pieces, GROUP, split_axis=0, concat_axis=0, tiled=True)]
    pallas_call x0 -> x1, Pallas kernels: none -> 17.3 us  [attend(): pl.pallas_call(attend_kernel, grid=(PIX,), out_shape=jax.ShapeDtypeStruct...]
  transfers between devices with their start and end apart: 3 -> 6, of which waited for: 3 -> 6; matrix products, arithmetic and copies ran while one was open for 1% -> 3% of each run, Pallas kernels for 0% -> 0%
where the time goes in v1:
time: 251 us
  waiting for transfers between devices  178 us (71%)
  blocking collectives  17.3 us (7%)
  Pallas kernels  17.3 us (7%)
  between operations  13.3 us (5%)
  starting transfers between devices  11.5 us (5%)
  local copies, waits for them, and re-layouts  8.45 us (3%)
  other arithmetic  5.05 us (2%)
    all_gather x4, waiting for transfers between devices, body(): lax.all_gather(w, 'pix', axis=0, tiled=False)  112 us
    all_gather x1, waiting for transfers between devices, body(): held = lax.all_gather(spread, 'z', axis=0, tiled=True)  33.7 us
    all_to_all x1, waiting for transfers between devices, body(): lax.all_to_all(outgoing, GROUP, split_axis=0, concat_axis=0, tiled=True)  29.8 us
    all_to_all x1, blocking collectives, body(): lax.all_to_all(pieces, GROUP, split_axis=0, concat_axis=0, tiled=True)  17.3 us
    pallas_call x1, Pallas kernels, attend(): pl.pallas_call(attend_kernel, grid=(PIX,), out_shape=jax.ShapeDtypeStruct...  17.3 us
    all_to_all x1, starting transfers between devices, body(): lax.all_to_all(outgoing, GROUP, split_axis=0, concat_axis=0, tiled=True)  11.4 us
  transfers between devices with their start and end apart: 6, of which 6 were waited for; matrix products, arithmetic and copies ran while one was open for 3% of the time, Pallas kernels for 0%

profile of v1, /device:TPU:1, one launch (start us, length us, event | category | flops | bytes accessed | tf_op | source)
XLA Modules:
  0.0 251.0 jit_solution(4252830928142389274)
XLA Ops:
  6.5 0.0 all-gather.10.cloned.1.call-start
  6.5 1.1 convert_reduce_fusion
  7.6 1.2 fusion.2
  8.8 1.2 fusion.3
  10.0 0.0 copy-start.2
  10.0 0.0 copy-start.3
  10.0 0.2 reshape.73
  10.2 17.3 %all_to_all.10 = bf16[32,16,256]{2,1,0:T(8,128)(2,1)} all-to-all(bf16[32,16,256]{2,1,0:T(8,128)(2,1)S(1)} %bitcast.27), channel_id=1, replica_groups=mesh['x'=4,'z'=8,'core'=2,'pix'=4] {'x','core','pix'}, dimensions={0} | all-to-all | bytes 524288 | tf_op jit(solution)/shard_map/all_to_all | solution.py:92
  27.5 0.0 all-gather.10.cloned.1.call-update
  27.5 0.0 all-gather.18.cloned.1.call-start
  27.6 0.7 all-gather.18.cloned.1.call-update
  28.3 0.0 all-gather.12.cloned.1.call-start
  28.3 0.7 all-gather.12.cloned.1.call-update
  29.0 0.0 all-gather.14.cloned.1.call-start
  29.1 0.5 all-gather.14.cloned.1.call-update
  29.6 0.0 all-gather.16.cloned.1.call-start
  29.6 0.5 all-gather.16.cloned.1.call-update
  30.2 0.0 copy-done.2
  30.2 0.0 copy-done.3
  30.2 0.1 reshape.71
  30.4 0.1 copy.31
  30.4 0.1 reshape.75
  30.5 0.1 copy.30
  30.6 0.1 copy.27
  30.7 33.7 %all-gather.10.cloned.1.call-done = bf16[256,16,256]{2,1,0:T(8,128)(2,1)} async-done(((bf16[32,16,256]{2,1,0:T(8,128)(2,1)}), bf16[256,16,256]{2,1,0:T(8,128)(2,1)}) %all-gather.10.cloned.1.call-update) | async-done | bytes 2097168 | tf_op jit(solution)/shard_map/all_gather | solution.py:93
  64.4 2.3 gather_fusion
  66.8 1.6 broadcast_select_fusion
  68.4 0.0 copy-start.4
  68.4 11.4 %all-to-all-start.1 = ((bf16[32,8,16,256]{3,2,1,0:T(8,128)(2,1)}), bf16[32,8,16,256]{3,2,1,0:T(8,128)(2,1)S(1)}, u32[]{:S(2)}, u32[]{:S(2)}) async-start(bf16[32,8,16,256]{3,2,1,0:T(8,128)(2,1)} %broadcast_select_fusion), calls=%async_computation.1 | async-start | bytes 4194304 | tf_op jit(solution)/shard_map/all_to_all | solution.py:99
  79.8 0.0 copy-done.4
  79.8 0.7 dynamic_slice.7.count_ref
  80.4 29.8 %all-to-all-done.1 = bf16[32,8,16,256]{3,2,1,0:T(8,128)(2,1)S(1)} async-done(((bf16[32,8,16,256]{3,2,1,0:T(8,128)(2,1)}), bf16[32,8,16,256]{3,2,1,0:T(8,128)(2,1)S(1)}, u32[]{:S(2)}, u32[]{:S(2)}) %all-to-all-start.1) | async-done | bytes 2097184 | tf_op jit(solution)/shard_map/all_to_all | solution.py:99
  110.3 2.7 %copy.29 = bf16[8,8,16,4,256]{4,3,2,1,0:T(4,128)(2,1)S(1)} copy(bf16[8,8,16,4,256]{4,2,0,3,1:T(8,128)(2,1)S(1)} %bitcast.24) | data formatting | bytes 4194304 | tf_op jit(solution)/shard_map/transpose | solution.py:100
  113.0 0.0 copy-start.1
  113.0 0.5 copy.32
  113.5 9.9 %all-gather.18.cloned.1.call-done = bf16[1024,1024]{1,0:T(8,128)(2,1)} async-done(((bf16[256,1024]{1,0:T(8,128)(2,1)}), bf16[1024,1024]{1,0:T(8,128)(2,1)}) %all-gather.18.cloned.1.call-update) | async-done | bytes 2097168 | tf_op jit(solution)/shard_map/all_gather | solution.py:94
  123.4 32.0 %all-gather.12.cloned.1.call-done = bf16[4096,256]{1,0:T(8,128)(2,1)} async-done(((bf16[1024,256]{1,0:T(8,128)(2,1)}), bf16[4096,256]{1,0:T(8,128)(2,1)}) %all-gather.12.cloned.1.call-update) | async-done | bytes 2097168 | tf_op jit(solution)/shard_map/all_gather | solution.py:94
  155.4 35.1 %all-gather.14.cloned.1.call-done = bf16[4096,256]{1,0:T(8,128)(2,1)} async-done(((bf16[1024,256]{1,0:T(8,128)(2,1)}), bf16[4096,256]{1,0:T(8,128)(2,1)}) %all-gather.14.cloned.1.call-update) | async-done | bytes 2097168 | tf_op jit(solution)/shard_map/all_gather | solution.py:94
  190.5 35.1 %all-gather.16.cloned.1.call-done = bf16[4096,256]{1,0:T(8,128)(2,1)} async-done(((bf16[1024,256]{1,0:T(8,128)(2,1)}), bf16[4096,256]{1,0:T(8,128)(2,1)}) %all-gather.16.cloned.1.call-update) | async-done | bytes 2097168 | tf_op jit(solution)/shard_map/all_gather | solution.py:94
  225.6 0.0 copy-done.1
  225.6 0.0 copy-start
  225.6 1.6 copy-done
  227.2 17.3 %shard_map.91 = bf16[128,1024]{1,0:T(8,128)(2,1)} custom-call(s32[1]{0:T(128)} %dynamic_slice.7.count_ref, bf16[128,1024]{1,0:T(8,128)(2,1)S(1)} %copy-done.1, bf16[1024,1024]{1,0:T(8,128)(2,1)S(1)} %bitcast.21, bf16[4,1024,256]{2,1,0:T(8,128)(2,1)S(1)} %bitcast.22, bf16[4,1024,256]{2,1,0:T(8,128)(2,1)} %bitcast.31, bf16[4,1024,256]{2,1,0:T(8,128)(2,1)} %bitcast.32, ...), custom_call_target="tpu_custom_call" | custom-call | flops 5400000000 | bytes 11534336 | tf_op jit(solution)/shard_map/pallas_call | solution.py:66
  (8 shorter events, 0.1 us)
Async XLA Ops:
  6.5 57.9 %all-gather.10.cloned.1.call-start = ((), (), s32[]{:S(2)}) async-start(), calls=%async_computation.2 | async-start | bytes 2359296 | tf_op jit(solution)/shard_map/all_gather | solution.py:93
  10.0 20.2 %copy-start.2 = (s32[256,8]{0,1:T(8,128)S(1)}, s32[256,8]{0,1:T(8,128)}, u32[]{:S(2)}) copy-start(s32[256,8]{0,1:T(8,128)} %param.16) | copy-start | bytes 24580
  10.0 20.2 %copy-start.3 = (s32[256,8]{0,1:T(8,128)S(1)}, s32[256,8]{0,1:T(8,128)}, u32[]{:S(2)}) copy-start(s32[256,8]{0,1:T(8,128)} %param.15) | copy-start | bytes 24580
  27.5 95.8 %all-gather.18.cloned.1.call-start = ((), (), s32[]{:S(2)}) async-start(), calls=%async_computation.6 | async-start | bytes 2621440 | tf_op jit(solution)/shard_map/all_gather | solution.py:94
  28.3 127.1 %all-gather.12.cloned.1.call-start = ((), (), s32[]{:S(2)}) async-start(), calls=%async_computation.3 | async-start | bytes 2621440 | tf_op jit(solution)/shard_map/all_gather | solution.py:94
  29.0 161.5 %all-gather.14.cloned.1.call-start = ((), (), s32[]{:S(2)}) async-start(), calls=%async_computation.4 | async-start | bytes 2621440 | tf_op jit(solution)/shard_map/all_gather | solution.py:94
  29.6 196.0 %all-gather.16.cloned.1.call-start = ((), (), s32[]{:S(2)}) async-start(), calls=%async_computation.5 | async-start | bytes 2621440 | tf_op jit(solution)/shard_map/all_gather | solution.py:94
  68.4 11.4 %copy-start.4 = (s32[4]{0:T(128)S(1)}, s32[4]{0:T(128)}, u32[]{:S(2)}) copy-start(s32[4]{0:T(128)} %param.17) | copy-start | bytes 52
  68.4 41.9 %all-to-all-start.1 = ((bf16[32,8,16,256]{3,2,1,0:T(8,128)(2,1)}), bf16[32,8,16,256]{3,2,1,0:T(8,128)(2,1)S(1)}, u32[]{:S(2)}, u32[]{:S(2)}) async-start(bf16[32,8,16,256]{3,2,1,0:T(8,128)(2,1)} %broadcast_select_fusion), calls=%async_computation.1 | async-start | bytes 4194304 | tf_op jit(solution)/shard_map/all_to_all | solution.py:99
  113.0 112.7 %copy-start.1 = (bf16[128,1024]{1,0:T(8,128)(2,1)S(1)}, bf16[128,1024]{1,0:T(8,128)(2,1)}, u32[]{:S(2)}) copy-start(bf16[128,1024]{1,0:T(8,128)(2,1)} %target_ref.1) | copy-start | bytes 786436
  225.6 1.6 copy-start
Sparse Core Ops, SparseCore 0:
  27.7 36.7 all-gather.9
  66.2 57.0 all-gather.17
  125.2 30.1 all-gather.11
  157.0 33.4 all-gather.13
  192.1 33.4 all-gather.15
